TPU v7x, 32 devices: a whole 2x2x4 slice. The times are simulated.
32 devices in a mesh: gx: 4 (over y, core), gy: 8 (over z, x).
Axes of the slice: x: 2, y: 2, z: 4, core: 2. Of those that a mesh axis runs over, the one named last changes fastest.
Arguments:
- velocity: float32 [3, 384, 256, 256], P(None, 'gx', 'gy'), may hold values from -6 to 6
- inflow: float32 [3, 256, 256], P(None, 'gy'), may hold values from -5 to 5
- positions: int32 [4, 64, 3, 256], P('gx'), may hold values from 0 to 381, as said below
- tiles: int32 [4, 64, 2], P('gx'), may hold values from 0 to 7, as said below
- coefs: float32 [4, 64, 256], P('gx'), may hold values from 2 to 20
- counts: int32 [4], P('gx'), may hold values from 1 to 64, as said below
Outputs:
- velocity_next: float32 [3, 384, 256, 256], P(None, 'gx', 'gy')
- blade_force: float32 [4, 64, 3, 256], P('gx')
Inputs may be any that keep to these rules, and one draw needn't show every extreme that they name: `positions`: for a record of tile row r, coordinate 0 is one value for all its points, from r * 96 + 2 to r * 96 + 93; coordinate 2 lies from 2 to 253; the points of a record lie on a straight segment in y and z. tiles[r, s, 1] is 2 or 3; the first listed y tile is the lowest y tile that holds a cell within 2 in y of some point of the record, or the tile after it. Records of row r with index below counts[r] are live; some row is full and some row has one live record.
All inputs are finite; a program needn't handle non-finite values.
Results may differ from a plain program's by a relative error of at most 0.00008.
Values sent between devices are 32-bit elements; how exact they have to be, the bound alone decides.
No kernel may reach another device: no remote copies, remote signals or barrier semaphores. Data moves between devices by JAX's collectives and lax.ppermute only.
A program may use at most 128 MiB of HBM per device.

v0:
```python
import jax
import jax.numpy as jnp
from jax import lax
from jax.sharding import PartitionSpec as P

REC_ROW = 64
RAD = 2


VISCOSITY = 0.05
TIME_STEP = 0.1
WIDTH_EPS = 1.5
ROOT_PI = 1.7724538509055159


def padded(block, sides, width, periodic):
    for axis, dim in sides:
        count = lax.axis_size(axis)
        forward = [(i, i + 1) for i in range(count - 1)]
        if periodic:
            forward.append((count - 1, 0))
        backward = [(target, source) for source, target in forward]
        low = lax.ppermute(
            lax.slice_in_dim(block, block.shape[dim] - width, None, axis=dim), axis, forward
        )
        high = lax.ppermute(lax.slice_in_dim(block, 0, width, axis=dim), axis, backward)
        block = jnp.concatenate([low, block, high], axis=dim)
    return block


def kernel_weight(offset):
    inside = jnp.abs(offset) <= RAD
    dist = offset.astype(jnp.float32)
    value = jnp.exp(-((dist / WIDTH_EPS) ** 2)) / (WIDTH_EPS * ROOT_PI)
    return jnp.where(inside, value, jnp.zeros_like(value))


def tendency(field, inflow, force):
    tile_x = lax.axis_index("gx")
    last_x = lax.axis_size("gx") - 1
    xhalo = padded(field, (("gx", 1),), 1, False)
    west_ghost = jnp.where(tile_x == 0, inflow[:, None], xhalo[:, :1])
    east_ghost = jnp.where(tile_x == last_x, field[:, -1:], xhalo[:, -1:])
    xpad = jnp.concatenate([west_ghost, field, east_ghost], axis=1)
    ypad = padded(field, (("gy", 2),), 1, True)
    zpad = jnp.pad(field, ((0, 0), (0, 0), (0, 0), (1, 1)))
    east, west = (xpad[:, 2:], xpad[:, :-2])
    north, south = (ypad[:, :, 2:], ypad[:, :, :-2])
    upper, lower = (zpad[:, :, :, 2:], zpad[:, :, :, :-2])
    advect = (
        field[0:1] * (east - west) * 0.5
        + field[1:2] * (north - south) * 0.5
        + field[2:3] * (upper - lower) * 0.5
    )
    diffuse = east + west + north + south + upper + lower - 6.0 * field
    return -advect + VISCOSITY * diffuse + force


def force_law(sampled, strength):
    speed_norm = jnp.sqrt(jnp.sum(sampled * sampled, axis=0))
    return -strength * speed_norm * sampled


def forcing(field, positions, tiles, coefs, counts):
    highest = lax.Precision.HIGHEST
    tile_x = lax.axis_index("gx")
    tile_y = lax.axis_index("gy")
    groups_y = lax.axis_size("gy")
    cells_x = field.shape[1]
    cells_y = field.shape[2]
    depth = field.shape[3]
    total_y = cells_y * groups_y
    record = positions[0]
    hub_x = record[:, 0, 0] - tile_x * cells_x
    point_y = record[:, 1, :]
    point_z = record[:, 2, :]
    first_tile = tiles[0, :, 0]
    tile_count = tiles[0, :, 1]
    listed = ((tile_y - first_tile) % groups_y < tile_count).astype(jnp.float32)
    along_x = kernel_weight(jnp.arange(cells_x, dtype=jnp.int32)[None, :] - hub_x[:, None])
    cell_y = tile_y * cells_y + jnp.arange(cells_y, dtype=jnp.int32)
    dist_y = (cell_y[None, :, None] - point_y[:, None, :] + total_y // 2) % total_y - total_y // 2
    along_y = kernel_weight(dist_y) * listed[:, None, None]
    along_z = kernel_weight(jnp.arange(depth, dtype=jnp.int32)[None, None, :] - point_z[:, :, None])
    planes = jnp.einsum("ri,cijk->rcjk", along_x, field, precision=highest)
    inner_sums = jnp.einsum("rcjk,rpk->rcjp", planes, along_z, precision=highest)
    partial_value = jnp.einsum("rcjp,rjp->crp", inner_sums, along_y, precision=highest)
    live_mask = (jnp.arange(REC_ROW, dtype=jnp.int32) < counts[0]).astype(jnp.float32)
    strength = coefs[0] * live_mask[:, None]
    sampled = lax.psum(partial_value, "gy")
    point_force = force_law(sampled, strength)
    weighted = along_y[None] * point_force[:, :, None, :]
    force_slab = jnp.einsum("crjp,rpk->rcjk", weighted, along_z, precision=highest)
    grid_force = jnp.einsum("ri,rcjk->cijk", along_x, force_slab, precision=highest)
    return (grid_force, point_force)


def local(velocity, inflow, positions, tiles, coefs, counts):
    force_a, points_a = forcing(velocity, positions, tiles, coefs, counts)
    section = velocity + TIME_STEP * tendency(velocity, inflow, force_a)
    force_b, points_b = forcing(section, positions, tiles, coefs, counts)
    velocity_next = 0.5 * (velocity + section + TIME_STEP * tendency(section, inflow, force_b))
    mean_force = 0.5 * (points_a + points_b)
    blade_force = mean_force.transpose(1, 0, 2)[None]
    return (velocity_next, blade_force)


def solution(mesh):
    return jax.shard_map(
        local,
        mesh=mesh,
        in_specs=(
            P(None, "gx", "gy", None),
            P(None, "gy", None),
            P("gx", None, None, None),
            P("gx", None, None),
            P("gx", None, None),
            P("gx"),
        ),
        out_specs=(P(None, "gx", "gy", None), P("gx", None, None, None)),
        check_vma=False,
    )
```

profile of v0, /device:TPU:0, one launch (start us, length us, event | category | flops | bytes accessed | tf_op | source)
XLA Modules:
  0.0 415.3 jit_solution(7301175528497762311)
XLA Ops:
  7.2 0.0 all-reduce.5.cloned.1.call-start
  7.2 0.9 slice.110
  8.1 0.1 copy.26
  8.2 1.3 collective-permute-start
  9.5 0.8 compare_convert_fusion.1
  10.3 0.9 slice_bitcast_fusion.7
  11.2 0.9 fusion.56
  12.1 15.0 %fusion.61 = f32[64,3,32,256]{3,0,2,1:T(8,128)S(1)} fusion(s32[64]{0:T(128)S(1)} %fusion.56, f32[3,96,32,256]{3,2,1,0:T(8,128)} %param.6), kind=kOutput, calls=%fused_computation.99 | convolution fusion | flops 1811994624 | bytes 15728896 | tf_op jit(solution)/shard_map/ri,cijk->rcjk/dot_general | solution.py:85
  27.1 3.2 select_multiply_fusion
  30.3 27.9 %multiply_reduce_fusion.1 = f32[64,256,3]{1,2,0:T(4,128)S(1)} fusion(f32[64,256,32]{1,2,0:T(8,128)S(1)} %get-tuple-element.25, s32[64,256]{1,0:T(8,128)S(1)} %get-tuple-element.23, f32[64,3,32,256]{3,0,2,1:T(8,128)S(1)} %fusion.61), kind=kOutput, calls=%fused_computation.57 | convolution fusion | flops 4872683520 | bytes 8650752 | tf_op jit(solution)/shard_map/rcjk,rpk->rcjp/dot_general | solution.py:86
  58.2 0.7 copy.91
  58.9 0.5 all-reduce.7.cloned.1.call-start
  59.4 9.1 %copy.38 = f32[3,96,32,256]{3,1,2,0:T(8,128)S(1)} copy(f32[3,96,32,256]{3,2,1,0:T(8,128)} %param.6) | data formatting | bytes 18874368 | tf_op args[0]
  68.6 1.0 fusion.124
  69.5 2.9 collective-permute-start.3
  72.5 6.0 %collective-permute-start.2 = (f32[3,96,1,256]{3,1,2,0:T(8,128)}, f32[3,96,1,256]{3,1,2,0:T(8,128)}, u32[]{:S(2)}, u32[]{:S(2)}) collective-permute-start(f32[3,96,1,256]{3,1,2,0:T(8,128)} %get-tuple-element.21), channel_id=1, source_target_pairs={{1,0},{2,1},{3,2},{4,3},{5,4},{6,5},{7,6},{0,7},{9,8},{10,9},{11,1... | collective-permute-start | bytes 884744 | tf_op jit(solution)/shard_map/ppermute | solution.py:26
  78.5 8.2 %slice_bitcast_fusion.5 = (f32[96,32,256]{2,1,0:T(8,128)}, f32[96,32,256]{2,1,0:T(8,128)}, f32[96,32,256]{2,1,0:T(8,128)S(1)}) fusion(f32[3,96,32,256]{3,2,1,0:T(8,128)} %param.6), kind=kLoop, calls=%fused_computation.69 | loop fusion | bytes 18874368 | tf_op jit(solution)/shard_map/mul | solution.py:51
  87.3 5.4 %copy.24 = f32[96,32,256]{2,0,1:T(8,128)} copy(f32[96,32,256]{2,1,0:T(8,128)} %get-tuple-element.15) | data formatting | bytes 6291456 | tf_op jit(solution)/shard_map/mul | solution.py:51
  92.7 5.4 %copy.34 = f32[96,32,256]{2,0,1:T(8,128)} copy(f32[96,32,256]{2,1,0:T(8,128)} %get-tuple-element.16) | data formatting | bytes 6291456 | tf_op jit(solution)/shard_map/mul | solution.py:53
  98.1 3.5 copy.29
  101.6 2.0 fusion.123
  103.6 3.5 collective-permute-start.1
  107.1 27.3 %all-reduce.5.cloned.1.call-done = f32[3,64,256]{2,1,0:T(8,128)} async-done(((f32[3,64,256]{2,1,0:T(8,128)}), f32[3,64,256]{2,1,0:T(8,128)}) %all-reduce.5.cloned.1.call-update) | async-done | bytes 196624 | tf_op jit(solution)/shard_map/psum | solution.py:90
  134.4 0.9 multiply_reduce_fusion.3
  135.4 0.1 fusion.55
  135.5 0.9 broadcast_multiply_fusion.3
  136.5 23.0 %fusion.4 = f32[64,3,32,256]{3,2,1,0:T(8,128)} fusion(s32[64,256]{1,0:T(8,128)} %copy-done.7, f32[3,64,256]{2,1,0:T(8,128)S(1)} %broadcast_multiply_fusion.3, f32[64,32,256]{2,1,0:T(8,128)} %get-tuple-element.24), kind=kOutput, calls=%fused_computation.4 | convolution fusion | flops 4871159808 | bytes 8650752 | tf_op jit(solution)/shard_map/crjp,rpk->rcjk/dot_general | solution.py:93
  159.4 0.1 broadcast_select_fusion.1
  159.6 38.5 %fusion.12 = f32[3,96,32,256]{3,1,2,0:T(8,128)} fusion(f32[3,96,32,256]{3,1,2,0:T(8,128)} %copy-done, f32[3,96,1,256]{3,1,2,0:T(8,128)} %collective-permute-done.2, f32[3,96,1,256]{3,1,2,0:T(8,128)} %collective-permute-done.3, f32[3,1,32,256]{3,1,2,0:T(1,128)} %get-tuple-element.19, f32[3,1,32,256]{3,1,2,0:T(1,128)S(1)} %broadcast_select_fusion.1, ...), kind=kOutput, calls=%fused_computation.28 | convolution fusion | flops 1873336320 | bytes 35389696 | tf_op jit(solution)/shard_map/ri,rcjk->cijk/dot_general | solution.py:94
  198.1 2.0 slice.147
  200.1 1.9 fusion.122
  202.0 8.8 %fusion.58 = f32[64,3,32,256]{3,0,2,1:T(8,128)S(1)} fusion(f32[3,96,32,256]{3,1,2,0:T(8,128)} %fusion.12, s32[64]{0:T(128)S(1)} %fusion.56), kind=kOutput, calls=%fused_computation.96 | convolution fusion | flops 1811994624 | bytes 15728896 | tf_op jit(solution)/shard_map/ri,cijk->rcjk/dot_general | solution.py:85
  210.8 3.6 slice_bitcast_fusion.2
  214.4 1.3 collective-permute-start.4
  215.6 0.8 collective-permute-start.7
  216.5 3.9 collective-permute-start.6
  220.4 28.8 %multiply_reduce_fusion = f32[64,256,3]{1,2,0:T(4,128)S(1)} fusion(f32[64,256,32]{1,2,0:T(8,128)} %copy-done.2, s32[64,256]{1,0:T(8,128)S(1)} %copy-done.8, f32[64,3,32,256]{3,0,2,1:T(8,128)S(1)} %fusion.58), kind=kOutput, calls=%fused_computation.52 | convolution fusion | flops 4872683520 | bytes 8650752 | tf_op jit(solution)/shard_map/rcjk,rpk->rcjp/dot_general | solution.py:86
  249.2 0.7 copy.90
  250.0 2.0 fusion.121
  251.9 3.3 collective-permute-start.5
  255.2 63.9 %all-reduce.7.cloned.1.call-done = f32[3,64,256]{2,1,0:T(8,128)} async-done(((f32[3,64,256]{2,1,0:T(8,128)}), f32[3,64,256]{2,1,0:T(8,128)}) %all-reduce.7.cloned.1.call-update) | async-done | bytes 196624 | tf_op jit(solution)/shard_map/psum | solution.py:90
  319.1 1.0 multiply_reduce_fusion.2
  320.1 0.9 fusion.54
  321.0 1.6 multiply_bitcast_fusion
  322.6 22.8 %fusion = f32[64,3,32,256]{3,2,1,0:T(8,128)} fusion(s32[64,256]{1,0:T(8,128)} %copy-done.7, f32[3,64,256]{2,1,0:T(8,128)S(1)} %get-tuple-element.7, f32[64,32,256]{2,1,0:T(8,128)} %get-tuple-element.24), kind=kOutput, calls=%fused_computation | convolution fusion | flops 4871159808 | bytes 8650752 | tf_op jit(solution)/shard_map/crjp,rpk->rcjk/dot_general | solution.py:93
  345.5 0.1 broadcast_select_fusion
  345.6 49.7 %fusion.10 = f32[3,96,32,256]{3,1,2,0:T(8,128)} fusion(f32[3,96,32,256]{3,1,2,0:T(8,128)} %fusion.12, f32[3,96,1,256]{3,1,2,0:T(8,128)} %collective-permute-done.6, f32[3,96,1,256]{3,1,2,0:T(8,128)} %collective-permute-done.7, f32[3,1,32,256]{3,1,2,0:T(1,128)S(1)} %copy-done.6, f32[3,1,32,256]{3,1,2,0:T(1,128)S(1)} %broadcast_select_fusion, ...), kind=kOutput, calls=%fused_computation.25 | convolution fusion | flops 1878054912 | bytes 44826880 | tf_op jit(solution)/shard_map/ri,rcjk->cijk/dot_general | solution.py:94
  395.3 12.9 %copy.39 = f32[3,96,32,256]{3,2,1,0:T(8,128)} copy(f32[3,96,32,256]{3,1,2,0:T(8,128)} %fusion.10) | data formatting | bytes 18874368
  (37 shorter events, 0.1 us)
Async XLA Ops:
  7.2 127.3 %all-reduce.5.cloned.1.call-start = ((), (), s32[]{:S(2)}) async-start(), calls=%async_computation | async-start | bytes 393216 | tf_op jit(solution)/shard_map/psum | solution.py:90
  8.2 93.4 %collective-permute-start = (f32[3,1,32,256]{3,1,2,0:T(1,128)S(1)}, f32[3,1,32,256]{3,1,2,0:T(1,128)S(1)}, u32[]{:S(2)}, u32[]{:S(2)}) collective-permute-start(f32[3,1,32,256]{3,1,2,0:T(1,128)S(1)} %copy.26), channel_id=1, source_target_pairs={{8,0},{16,8},{24,16},{9,1},{17,9},{25,17},{10,2},{18,10},{26,18},{... | collective-permute-start | bytes 294920 | tf_op jit(solution)/shard_map/ppermute | solution.py:26
  11.2 19.1 %copy-start.7 = (s32[64,256]{1,0:T(8,128)}, s32[64,256]{1,0:T(8,128)S(1)}, u32[]{:S(2)}) copy-start(s32[64,256]{1,0:T(8,128)S(1)} %get-tuple-element.23) | copy-start | bytes 196612
  30.3 27.9 %copy-start.2 = (f32[64,256,32]{1,2,0:T(8,128)}, f32[64,256,32]{1,2,0:T(8,128)S(1)}, u32[]{:S(2)}) copy-start(f32[64,256,32]{1,2,0:T(8,128)S(1)} %get-tuple-element.25) | copy-start | bytes 6291460
  58.9 260.2 %all-reduce.7.cloned.1.call-start = ((), (), s32[]{:S(2)}) async-start(), calls=%async_computation.1 | async-start | bytes 393216 | tf_op jit(solution)/shard_map/psum | solution.py:90
  68.6 3.9 copy-start
  69.5 90.0 %collective-permute-start.3 = (f32[3,96,1,256]{3,1,2,0:T(8,128)}, f32[3,96,1,256]{3,1,2,0:T(8,128)}, u32[]{:S(2)}, u32[]{:S(2)}) collective-permute-start(f32[3,96,1,256]{3,1,2,0:T(8,128)} %get-tuple-element.20), channel_id=1, source_target_pairs={{0,1},{1,2},{2,3},{3,4},{4,5},{5,6},{6,7},{7,0},{8,9},{9,10},{10,1... | collective-permute-start | bytes 884744 | tf_op jit(solution)/shard_map/ppermute | solution.py:23
  72.5 87.1 %collective-permute-start.2 = (f32[3,96,1,256]{3,1,2,0:T(8,128)}, f32[3,96,1,256]{3,1,2,0:T(8,128)}, u32[]{:S(2)}, u32[]{:S(2)}) collective-permute-start(f32[3,96,1,256]{3,1,2,0:T(8,128)} %get-tuple-element.21), channel_id=1, source_target_pairs={{1,0},{2,1},{3,2},{4,3},{5,4},{6,5},{7,6},{0,7},{9,8},{10,9},{11,1... | collective-permute-start | bytes 884744 | tf_op jit(solution)/shard_map/ppermute | solution.py:26
  87.3 48.1 %copy-start.5 = (f32[1,64,256]{2,1,0:T(8,128)S(1)}, f32[1,64,256]{2,1,0:T(8,128)}, u32[]{:S(2)}) copy-start(f32[1,64,256]{2,1,0:T(8,128)} %param.10) | copy-start | bytes 196612
  103.6 55.9 %collective-permute-start.1 = (f32[3,1,32,256]{3,1,2,0:T(1,128)}, f32[3,1,32,256]{3,1,2,0:T(1,128)}, u32[]{:S(2)}, u32[]{:S(2)}) collective-permute-start(f32[3,1,32,256]{3,1,2,0:T(1,128)} %get-tuple-element.18), channel_id=1, source_target_pairs={{0,8},{8,16},{16,24},{1,9},{9,17},{17,25},{2,10},{10,18},{18,26},{... | collective-permute-start | bytes 294920 | tf_op jit(solution)/shard_map/ppermute | solution.py:23
  136.4 23.0 %copy-start.4 = (f32[3,32,256]{2,1,0:T(8,128)S(1)}, f32[3,32,256]{2,1,0:T(8,128)}, u32[]{:S(2)}) copy-start(f32[3,32,256]{2,1,0:T(8,128)} %param.7) | copy-start | bytes 294916
  136.5 23.1 %copy-start.1 = (f32[96,32,256]{2,0,1:T(8,128)S(1)}, f32[96,32,256]{2,0,1:T(8,128)}, u32[]{:S(2)}) copy-start(f32[96,32,256]{2,0,1:T(8,128)} %copy.24) | copy-start | bytes 9437188
  198.1 12.7 %slice-start = ((s8[9437184]{0:T(1024)(128)(4,1)}), s8[4194304]{0:T(1024)(128)(4,1)S(1)}, s32[]{:S(2)}) async-start(s8[9437184]{0:T(1024)(128)(4,1)} %bitcast.95), calls=%async_computation.2 | async-start | bytes 8388608
  202.0 8.8 %slice-start.1 = ((s8[9437184]{0:T(1024)(128)(4,1)}), s8[4194304]{0:T(1024)(128)(4,1)S(1)}, s32[]{:S(2)}) async-start(s8[9437184]{0:T(1024)(128)(4,1)} %bitcast.95), calls=%async_computation.3 | async-start | bytes 8388608
  202.0 8.8 %slice-start.2 = ((s8[9437184]{0:T(1024)(128)(4,1)}), s8[1048576]{0:T(1024)(128)(4,1)S(1)}, s32[]{:S(2)}) async-start(s8[9437184]{0:T(1024)(128)(4,1)} %bitcast.95), calls=%async_computation.4 | async-start | bytes 2097152
  210.8 9.6 %copy-start.8 = (s32[64,256]{1,0:T(8,128)S(1)}, s32[64,256]{1,0:T(8,128)}, u32[]{:S(2)}) copy-start(s32[64,256]{1,0:T(8,128)} %copy-done.7) | copy-start | bytes 196612
  214.4 35.6 %collective-permute-start.4 = (f32[3,1,32,256]{3,1,2,0:T(1,128)}, f32[3,1,32,256]{3,1,2,0:T(1,128)}, u32[]{:S(2)}, u32[]{:S(2)}) collective-permute-start(f32[3,1,32,256]{3,1,2,0:T(1,128)} %slice.147), channel_id=1, source_target_pairs={{8,0},{16,8},{24,16},{9,1},{17,9},{25,17},{10,2},{18,10},{26,18},{... | collective-permute-start | bytes 294920 | tf_op jit(solution)/shard_map/ppermute | solution.py:26
  215.6 129.9 %collective-permute-start.7 = (f32[3,96,1,256]{3,1,2,0:T(8,128)}, f32[3,96,1,256]{3,1,2,0:T(8,128)}, u32[]{:S(2)}, u32[]{:S(2)}) collective-permute-start(f32[3,96,1,256]{3,1,2,0:T(8,128)} %get-tuple-element.13), channel_id=1, source_target_pairs={{0,1},{1,2},{2,3},{3,4},{4,5},{5,6},{6,7},{7,0},{8,9},{9,10},{10,1... | collective-permute-start | bytes 884744 | tf_op jit(solution)/shard_map/ppermute | solution.py:23
  216.5 104.5 %copy-start.3 = (f32[3,64,256]{2,1,0:T(8,128)S(1)}, f32[3,64,256]{2,1,0:T(8,128)}, u32[]{:S(2)}) copy-start(f32[3,64,256]{2,1,0:T(8,128)} %all-reduce.5.cloned.1.call-done) | copy-start | bytes 589828
  216.5 129.1 %collective-permute-start.6 = (f32[3,96,1,256]{3,1,2,0:T(8,128)}, f32[3,96,1,256]{3,1,2,0:T(8,128)}, u32[]{:S(2)}, u32[]{:S(2)}) collective-permute-start(f32[3,96,1,256]{3,1,2,0:T(8,128)} %get-tuple-element.14), channel_id=1, source_target_pairs={{1,0},{2,1},{3,2},{4,3},{5,4},{6,5},{7,6},{0,7},{9,8},{10,9},{11,1... | collective-permute-start | bytes 884744 | tf_op jit(solution)/shard_map/ppermute | solution.py:26
  251.9 93.5 %collective-permute-start.5 = (f32[3,1,32,256]{3,1,2,0:T(1,128)}, f32[3,1,32,256]{3,1,2,0:T(1,128)}, u32[]{:S(2)}, u32[]{:S(2)}) collective-permute-start(f32[3,1,32,256]{3,1,2,0:T(1,128)} %get-tuple-element.11), channel_id=1, source_target_pairs={{0,8},{8,16},{16,24},{1,9},{9,17},{17,25},{2,10},{10,18},{18,26},{... | collective-permute-start | bytes 294920 | tf_op jit(solution)/shard_map/ppermute | solution.py:23
  322.6 23.0 %copy-start.6 = (f32[3,1,32,256]{3,1,2,0:T(1,128)S(1)}, f32[3,1,32,256]{3,1,2,0:T(1,128)}, u32[]{:S(2)}) copy-start(f32[3,1,32,256]{3,1,2,0:T(1,128)} %get-tuple-element.12) | copy-start | bytes 294916
Sparse Core Ops, SparseCore 0:
  59.0 75.3 all-reduce.4
  250.1 68.9 all-reduce.6
where the time goes:
time: 423 us; the launch traced here: 415 us
  matrix products  214 us (51%)
  waiting for transfers between devices  91.3 us (22%)
  local copies, waits for them, and re-layouts  56.3 us (13%)
  starting transfers between devices  23.6 us (6%)
  between operations  15.2 us (4%)
  other arithmetic  14.5 us (3%)
    psum x2, waiting for transfers between devices, forcing(): sampled = lax.psum(partial_value, 'gy')  91.2 us
    dot_general x2, matrix products, forcing(): jnp.einsum('ri,rcjk->cijk', along_x, force_slab, precision=highest)  88.2 us
    dot_general x2, matrix products, forcing(): jnp.einsum('rcjk,rpk->rcjp', planes, along_z, precision=highest)  56.6 us
    dot_general x2, matrix products, forcing(): jnp.einsum('crjp,rpk->rcjk', weighted, along_z, precision=highest)  45.8 us
    dot_general x2, matrix products, forcing(): planes = jnp.einsum('ri,cijk->rcjk', along_x, field, precision=highest)  23.7 us
    unnamed x26, local copies, waits for them, and re-layouts  22.1 us
    mul x3, local copies, waits for them, and re-layouts, tendency(): field[0:1] * (east - west) * 0.5 + field[1:2] * (north - south) * 0.5  17.1 us
    ppermute x4, starting transfers between devices, padded(): lax.ppermute(lax.slice_in_dim(block, 0, width, axis=dim), axis, backward)  12.5 us
  transfers between devices with their start and end apart: 10, of which 2 were waited for; matrix products, arithmetic and copies ran while one was open for 40% of the time, Pallas kernels for 0%

commit v1 on v0

v1 whole, which is shorter than its diff:
```python
import functools
import math

import jax
import jax.numpy as jnp
from jax import lax
from jax.experimental import pallas as pl
from jax.experimental.pallas import tpu as pltpu
from jax.sharding import PartitionSpec as P

RAD = 2
VISCOSITY = 0.05
TIME_STEP = 0.1
WIDTH_EPS = 1.5
ROOT_PI = 1.7724538509055159
TAP = [math.exp(-((d / WIDTH_EPS) ** 2)) / (WIDTH_EPS * ROOT_PI) for d in range(RAD + 1)]
LANES = 128
SUB = 8
VMEM_LIMIT = 14 * 2**20

WHOLE = pl.BlockSpec(memory_space=pltpu.VMEM)
SCALAR = pl.BlockSpec(memory_space=pltpu.SMEM)
ANYWHERE = pl.BlockSpec(memory_space=pl.ANY)


def params(limit=VMEM_LIMIT):
    return pltpu.CompilerParams(vmem_limit_bytes=limit)


def cost(flops, nbytes):
    return pl.CostEstimate(flops=flops, bytes_accessed=nbytes, transcendentals=0)


def resident(x):
    return pltpu.with_memory_space_constraint(x, pltpu.VMEM)


def smooth_z(x):
    depth = x.shape[-1]
    near = pltpu.roll(x, 1, 1) + pltpu.roll(x, depth - 1, 1)
    far = pltpu.roll(x, 2, 1) + pltpu.roll(x, depth - 2, 1)
    return TAP[0] * x + TAP[1] * near + TAP[2] * far


def split(x):
    high = x.astype(jnp.bfloat16)
    low = (x - high.astype(jnp.float32)).astype(jnp.bfloat16)
    return jnp.concatenate([high, low], axis=0)


def one_hot(point_z, depth):
    cell = lax.broadcasted_iota(jnp.int32, (depth, point_z.shape[-1]), 0)
    return jnp.where(cell == point_z, 1.0, 0.0).astype(jnp.bfloat16)


def along_y(point_y, base, cells_y, total_y):
    near = point_y - base
    near = jnp.where(near > total_y // 2, near - total_y, near)
    near = jnp.where(near < -(total_y // 2), near + total_y, near)
    dist = jnp.abs(lax.broadcasted_iota(jnp.int32, (cells_y, point_y.shape[-1]), 0) - near)
    return jnp.where(
        dist == 0, TAP[0], jnp.where(dist == 1, TAP[1], jnp.where(dist == 2, TAP[2], 0.0))
    )


def record_list(tiles, counts, active):
    tile_y, groups_y = lax.axis_index("gy"), lax.axis_size("gy")

    def step(r, found):
        offset = tile_y - tiles[r, 0]
        offset = jnp.where(offset < 0, offset + groups_y, offset)
        keep = jnp.logical_and(offset < tiles[r, 1], r < counts[0])

        @pl.when(keep)
        def _():
            active[1 + found] = r

        return found + keep.astype(jnp.int32)

    active[0] = lax.fori_loop(0, tiles.shape[0], step, jnp.int32(0))


def for_pairs(active, body):
    found = active[0]

    def step(t, carry):
        first = 2 * t
        second = jnp.minimum(first + 1, found - 1)
        body(active[1 + first], active[1 + second], first + 1 < found)
        return carry

    lax.fori_loop(0, (found + 1) // 2, step, 0)


def sample_record(field, positions, hubs, partial, r):
    cells_x, cells_y, depth = field.shape[1:]
    total_y = cells_y * lax.axis_size("gy")
    hub = hubs[r] - lax.axis_index("gx") * cells_x
    base = lax.axis_index("gy") * cells_y
    planes = []
    for c in range(3):
        plane = TAP[0] * field[c, hub]
        plane += TAP[1] * (field[c, hub - 1] + field[c, hub + 1])
        plane += TAP[2] * (field[c, hub - 2] + field[c, hub + 2])
        planes.append(plane)
    planes = smooth_z(jnp.concatenate(planes, axis=0))
    pos = positions[r]
    picked = jnp.dot(
        split(planes), one_hot(pos[2:3], depth), preferred_element_type=jnp.float32
    )
    picked = picked[: 3 * cells_y] + picked[3 * cells_y :]
    weight = along_y(pos[1:2], base, cells_y, total_y)
    rows = [
        jnp.sum(picked[c * cells_y : (c + 1) * cells_y] * weight, axis=0, keepdims=True)
        for c in range(3)
    ]
    partial[r] = jnp.concatenate(rows, axis=0)


def sample_all(field, positions, hubs, active, partial):
    partial[...] = jnp.zeros_like(partial)

    def body(first, second, both):
        sample_record(field, positions, hubs, partial, first)
        sample_record(field, positions, hubs, partial, second)

    for_pairs(active, body)


def load_sample(velocity, positions, hubs, tiles, counts, field, partial, active, sem):
    copy = pltpu.make_async_copy(velocity, field, sem)
    copy.start()
    record_list(tiles, counts, active)
    copy.wait()
    sample_all(field, positions, hubs, active, partial)


def sample(field, positions, hubs, active, partial):
    sample_all(field, positions, hubs, active, partial)


def force_law(sampled, strength):
    speed = jnp.sqrt(jnp.sum(sampled * sampled, axis=0, keepdims=True))
    return -strength * speed * sampled


def slab_of(positions, coefs, own, low, high, cells_y, depth, scale, r):
    total_y = cells_y * lax.axis_size("gy")
    base = lax.axis_index("gy") * cells_y
    pos = positions[r]
    force = force_law(own[r] + (low[r] + high[r]), coefs[r] * scale)
    weight = along_y(pos[1:2], base, cells_y, total_y)
    spread = jnp.concatenate([weight * force[c : c + 1] for c in range(3)], axis=0)
    slab = lax.dot_general(
        split(spread),
        one_hot(pos[2:3], depth),
        (((1,), (1,)), ((), ())),
        preferred_element_type=jnp.float32,
    )
    return smooth_z(slab[: 3 * cells_y] + slab[3 * cells_y :])


def add_slab(field, slab, hub, cells_y):
    for c in range(3):
        part = slab[c * cells_y : (c + 1) * cells_y]
        terms = [tap * part for tap in TAP]
        for d in range(-RAD, RAD + 1):
            field[c, hub + d] = field[c, hub + d] + terms[abs(d)]


def spread_all(field, positions, hubs, active, coefs, own, low, high, scale):
    cells_x, cells_y, depth = field.shape[1:]
    start = lax.axis_index("gx") * cells_x

    def body(first, second, both):
        slab = functools.partial(slab_of, positions, coefs, own, low, high, cells_y, depth)
        slab_a = slab(scale, first)
        slab_b = slab(jnp.where(both, scale, 0.0), second)
        add_slab(field, slab_a, hubs[first] - start, cells_y)
        add_slab(field, slab_b, hubs[second] - start, cells_y)

    for_pairs(active, body)


def spread_section(field_in, positions, hubs, active, coefs, own, low, high, field, edge_x, edge_y):
    spread_all(field, positions, hubs, active, coefs, own, low, high, TIME_STEP)
    cells_x, cells_y, depth = field.shape[1:]
    for c in range(3):
        edge_x[0, c] = field[c, 0]
        edge_x[1, c] = field[c, cells_x - 1]

    def step(t, carry):
        for c in range(3):
            for k in range(SUB):
                i = t * SUB + k
                edge_y[0, c, i] = field[c, i, pl.ds(0, 1), :]
                edge_y[1, c, i] = field[c, i, pl.ds(cells_y - 1, 1), :]
        return carry

    lax.fori_loop(0, cells_x // SUB, step, 0)


def spread_next(
    field_in, positions, hubs, active, coefs, own, low, high, field, result, sem
):
    spread_all(field, positions, hubs, active, coefs, own, low, high, 0.5 * TIME_STEP)
    copy = pltpu.make_async_copy(field, result, sem)
    copy.start()
    copy.wait()


def advance(i, factor, field, west, east, south, north, emit):
    cells_y, depth = field.shape[2:]
    groups, halves = cells_y // SUB, depth // LANES
    row = lax.broadcasted_iota(jnp.int32, (SUB, LANES), 0)
    lane = lax.broadcasted_iota(jnp.int32, (SUB, LANES), 1)
    first_row, last_row = row == 0, row == SUB - 1
    first_lane, last_lane = lane == 0, lane == LANES - 1
    spread = factor * TIME_STEP * VISCOSITY
    centre = factor * (1.0 - 6.0 * TIME_STEP * VISCOSITY)
    zero = jnp.zeros((SUB, LANES), jnp.float32)

    def cut(h):
        return pl.ds(h * LANES, LANES)

    for g in range(groups):
        rows = pl.ds(g * SUB, SUB)
        q = [[field[c, i, rows, cut(h)] for h in range(halves)] for c in range(3)]
        coef = []
        for h in range(halves):
            speeds = [(0.5 * factor * TIME_STEP) * q[c][h] for c in range(3)]
            coef.append([(spread - s, spread + s) for s in speeds])
        for c in range(3):
            up = [pltpu.roll(q[c][h], LANES - 1, 1) for h in range(halves)]
            down = [pltpu.roll(q[c][h], 1, 1) for h in range(halves)]
            for h in range(halves):
                x = q[c][h]
                upper = jnp.where(last_lane, up[h + 1] if h + 1 < halves else zero, up[h])
                lower = jnp.where(first_lane, down[h - 1] if h > 0 else zero, down[h])
                if g + 1 < groups:
                    after = pltpu.roll(field[c, i, pl.ds((g + 1) * SUB, SUB), cut(h)], SUB - 1, 0)
                else:
                    after = jnp.broadcast_to(north[c, i, :, cut(h)], (SUB, LANES))
                if g > 0:
                    before = pltpu.roll(field[c, i, pl.ds((g - 1) * SUB, SUB), cut(h)], 1, 0)
                else:
                    before = jnp.broadcast_to(south[c, i, :, cut(h)], (SUB, LANES))
                above = jnp.where(last_row, after, pltpu.roll(x, SUB - 1, 0))
                below = jnp.where(first_row, before, pltpu.roll(x, 1, 0))
                (xe, xw), (yn, ys), (zu, zl) = coef[h]
                total = centre * x
                total += east(c, rows, cut(h)) * xe + west(c, rows, cut(h)) * xw
                total += above * yn + below * ys
                total += upper * zu + lower * zl
                emit(c, rows, cut(h), total)


def advance_all(factor, field, inflow, ghost_low, ghost_high, south, north, edge, emit):
    cells_x = field.shape[1]
    is_first = lax.axis_index("gx") == 0
    is_last = lax.axis_index("gx") == lax.axis_size("gx") - 1
    for c in range(3):
        edge[0, c] = jnp.where(is_first, inflow[c], ghost_low[c])
        edge[1, c] = jnp.where(is_last, field[c, cells_x - 1], ghost_high[c])

    def inner(i):
        return lambda c, rows, cols: field[c, i, rows, cols]

    def outer(side):
        return lambda c, rows, cols: edge[side, c, rows, cols]

    def one(i, west, east):
        advance(i, factor, field, west, east, south, north, functools.partial(emit, i))

    one(0, outer(0), inner(1))

    def step(i, carry):
        one(i, inner(i - 1), inner(i + 1))
        return carry

    lax.fori_loop(1, cells_x - 1, step, 0)
    one(cells_x - 1, inner(cells_x - 2), outer(1))


def advance_first(field, inflow, ghost_low, ghost_high, south, north, section, edge):
    def emit(i, c, rows, cols, value):
        section[c, i, rows, cols] = value

    advance_all(1.0, field, inflow, ghost_low, ghost_high, south, north, edge, emit)


def advance_second(
    section, field, inflow, ghost_low, ghost_high, south, north, result, edge
):
    def emit(i, c, rows, cols, value):
        result[c, i, rows, cols] = value + 0.5 * field[c, i, rows, cols]

    advance_all(0.5, section, inflow, ghost_low, ghost_high, south, north, edge, emit)


def shifted(x, axis, step, periodic):
    count = lax.axis_size(axis)
    pairs = [(i, (i + step) % count) for i in range(count)]
    if not periodic:
        pairs = [(s, t) for s, t in pairs if t - s == step]
    return lax.ppermute(x, axis, pairs)


def local(velocity, inflow, positions, tiles, coefs, counts):
    f32 = jnp.float32
    _, cells_x, cells_y, depth = velocity.shape
    groups_y = lax.axis_size("gy")
    positions, tiles, coefs = positions[0], tiles[0], coefs[0]
    records, _, points = positions.shape
    hubs = positions[:, 0, 0]
    strengths = coefs[:, None]
    whole = velocity.shape
    size = 4 * math.prod(whole)
    held = pltpu.VMEM(whole, f32)
    partial_shape = jax.ShapeDtypeStruct((records, 3, points), f32)

    west = shifted(velocity[:, -1], "gx", 1, False)
    east = shifted(velocity[:, 0], "gx", -1, False)
    south = shifted(velocity[:, :, -1:], "gy", 1, True)
    north = shifted(velocity[:, :, :1], "gy", -1, True)

    field, partial_a, active = pl.pallas_call(
        load_sample,
        out_shape=(held, partial_shape, jax.ShapeDtypeStruct((records + 1,), jnp.int32)),
        in_specs=[ANYWHERE, WHOLE, SCALAR, SCALAR, SCALAR],
        out_specs=(WHOLE, WHOLE, SCALAR),
        scratch_shapes=[pltpu.SemaphoreType.DMA],
        compiler_params=params(),
        cost_estimate=cost(2 * 10**9, 4 * size),
        name="load_sample",
    )(velocity, positions, hubs, tiles, counts)
    low_a = shifted(partial_a, "gy", 1, True)
    high_a = shifted(partial_a, "gy", -1, True)

    edge = pltpu.VMEM((2, 3, cells_y, depth), f32)
    section = pl.pallas_call(
        advance_first,
        out_shape=held,
        in_specs=[WHOLE] * 6,
        out_specs=WHOLE,
        scratch_shapes=[edge],
        compiler_params=params(),
        cost_estimate=cost(10**9, 4 * size),
        name="advance_first",
    )(resident(field), inflow, west, east, south, north)

    section, edge_x, edge_y = pl.pallas_call(
        spread_section,
        out_shape=(
            held,
            jax.ShapeDtypeStruct((2, 3, cells_y, depth), f32),
            jax.ShapeDtypeStruct((2, 3, cells_x, 1, depth), f32),
        ),
        in_specs=[WHOLE, WHOLE, SCALAR, SCALAR, WHOLE, WHOLE, WHOLE, WHOLE],
        out_specs=(WHOLE, WHOLE, WHOLE),
        input_output_aliases={0: 0},
        compiler_params=params(),
        cost_estimate=cost(2 * 10**9, 4 * size),
        name="spread_section",
    )(resident(section), positions, hubs, active, strengths, partial_a, low_a, high_a)

    west_b = shifted(edge_x[1], "gx", 1, False)
    east_b = shifted(edge_x[0], "gx", -1, False)
    south_b = shifted(edge_y[1], "gy", 1, True)
    north_b = shifted(edge_y[0], "gy", -1, True)

    partial_b = pl.pallas_call(
        sample,
        out_shape=partial_shape,
        in_specs=[WHOLE, WHOLE, SCALAR, SCALAR],
        out_specs=WHOLE,
        compiler_params=params(),
        cost_estimate=cost(2 * 10**9, 4 * size),
        name="sample",
    )(resident(section), positions, hubs, active)
    low_b = shifted(partial_b, "gy", 1, True)
    high_b = shifted(partial_b, "gy", -1, True)

    share = records // groups_y
    both = jnp.stack([partial_a, partial_b]).reshape(2, groups_y, share, 3, points)
    both = jnp.sum(lax.all_to_all(both, "gy", 1, 1), axis=1)
    mine = lax.axis_index("gy") * share
    live = (mine + jnp.arange(share, dtype=jnp.int32) < counts[0]).astype(f32)
    strength = lax.dynamic_slice_in_dim(coefs, mine, share, 0) * live[:, None]
    speed = jnp.sqrt(jnp.sum(both * both, axis=2, keepdims=True))
    mean_force = 0.5 * jnp.sum(-strength[None, :, None] * speed * both, axis=0)
    blade_force = lax.all_gather(mean_force, "gy", axis=0, tiled=True)

    following = pl.pallas_call(
        advance_second,
        out_shape=held,
        in_specs=[WHOLE] * 7,
        out_specs=WHOLE,
        scratch_shapes=[edge],
        compiler_params=params(),
        cost_estimate=cost(10**9, 4 * size),
        name="advance_second",
    )(resident(section), resident(field), inflow, west_b, east_b, south_b, north_b)

    _, velocity_next = pl.pallas_call(
        spread_next,
        out_shape=(held, jax.ShapeDtypeStruct(whole, f32)),
        in_specs=[WHOLE, WHOLE, SCALAR, SCALAR, WHOLE, WHOLE, WHOLE, WHOLE],
        out_specs=(WHOLE, ANYWHERE),
        input_output_aliases={0: 0},
        scratch_shapes=[pltpu.SemaphoreType.DMA],
        compiler_params=params(),
        cost_estimate=cost(2 * 10**9, 4 * size),
        name="spread_next",
    )(resident(following), positions, hubs, active, strengths, partial_b, low_b, high_b)
    return (velocity_next, blade_force[None])


def solution(mesh):
    return jax.shard_map(
        local,
        mesh=mesh,
        in_specs=(
            P(None, "gx", "gy", None),
            P(None, "gy", None),
            P("gx", None, None, None),
            P("gx", None, None),
            P("gx", None, None),
            P("gx"),
        ),
        out_specs=(P(None, "gx", "gy", None), P("gx", None, None, None)),
        check_vma=False,
    )
```

time: 423 us -> 159 us (0.38); the launches traced: 415 us -> 162 us
  matrix products: 214 us -> 0 us
  waiting for transfers between devices: 91.3 us -> 6.36 us
  Pallas kernels: 0 us -> 56.3 us
  blocking collectives: 0 us -> 32.6 us
  local copies, waits for them, and re-layouts: 56.3 us -> 30.2 us
  between operations: 15.2 us -> 1.55 us
  other arithmetic: 14.5 us -> 0.94 us
  starting transfers between devices: 23.6 us -> 34 us
    dot_general x8 -> x0, matrix products: 214 us -> none  [the longest x2 88.2 us: forcing(): jnp.einsum('ri,rcjk->cijk', along_x, force_slab, precision=highest)]
    psum x2 -> x0, waiting for transfers between devices: 91.2 us -> none  [forcing(): sampled = lax.psum(partial_value, 'gy')]
    pallas_call x0 -> x6, Pallas kernels: none -> 56.3 us  [the longest x1 11.8 us: local(): pl.pallas_call(advance_second, out_shape=held, in_specs=[WHOLE] * 7, out_...]
    all_gather x0 -> x1, blocking collectives: none -> 32.6 us  [local(): blade_force = lax.all_gather(mean_force, 'gy', axis=0, tiled=True)]
    mul x5 -> x0, local copies, waits for them, and re-layouts: 26 us -> none  [the longest x3 17.1 us: tendency(): field[0:1] * (east - west) * 0.5 + field[1:2] * (north - south) * 0.5]
    all_to_all x0 -> x1, starting transfers between devices: none -> 8.07 us  [local(): both = jnp.sum(lax.all_to_all(both, 'gy', 1, 1), axis=1)]
    ppermute x8 -> x12, waiting for transfers between devices: 0.02 us -> 6.35 us  [shifted(): return lax.ppermute(x, axis, pairs)]
    mul x4 -> x2, other arithmetic: 5.17 us -> 0.02 us  [local(): mean_force = 0.5 * jnp.sum(-strength[None, :, None] * speed * both, axis=0)]
  transfers between devices with their start and end apart: 10 -> 13, of which waited for: 2 -> 4; matrix products, arithmetic and copies ran while one was open for 40% -> 5% of each run, Pallas kernels for 0% -> 30%
where the time goes in v1:
time: 159 us; the launch traced here: 162 us
  Pallas kernels  56.3 us (35%)
  starting transfers between devices  34 us (21%)
  blocking collectives  32.6 us (21%)
  local copies, waits for them, and re-layouts  30.2 us (19%)
  waiting for transfers between devices  6.36 us (4%)
    all_gather x1, blocking collectives, local(): blade_force = lax.all_gather(mean_force, 'gy', axis=0, tiled=True)  32.6 us
    ppermute x12, starting transfers between devices, shifted(): return lax.ppermute(x, axis, pairs)  26 us
    unnamed x18, local copies, waits for them, and re-layouts  23.8 us
    pallas_call x1, Pallas kernels, local(): pl.pallas_call(advance_second, out_shape=held, in_specs=[WHOLE] * 7, out_...  11.8 us
    pallas_call x1, Pallas kernels, local(): pl.pallas_call(advance_first, out_shape=held, in_specs=[WHOLE] * 6, out_s...  11.6 us
    pallas_call x1, Pallas kernels, local(): pl.pallas_call(spread_next, out_shape=(held, jax.ShapeDtypeStruct(whole,...  11 us
    pallas_call x1, Pallas kernels, local(): pl.pallas_call(load_sample, out_shape=(held, partial_shape, jax.ShapeDtyp...  8.52 us
    all_to_all x1, starting transfers between devices, local(): both = jnp.sum(lax.all_to_all(both, 'gy', 1, 1), axis=1)  8.07 us
  transfers between devices with their start and end apart: 13, of which 4 were waited for; matrix products, arithmetic and copies ran while one was open for 5% of the time, Pallas kernels for 30%

profile of v1, /device:TPU:0, one launch (start us, length us, event | category | flops | bytes accessed | tf_op | source)
XLA Modules:
  0.0 162.1 jit_solution(6787008906246273282)
XLA Ops:
  0.6 1.0 slice_bitcast_fusion.4
  1.6 2.4 %collective-permute-start = (f32[3,32,256]{2,1,0:T(8,128)S(1)}, f32[3,32,256]{2,1,0:T(8,128)S(1)}, u32[]{:S(2)}, u32[]{:S(2)}) collective-permute-start(f32[3,32,256]{2,1,0:T(8,128)S(1)} %get-tuple-element.19), channel_id=1, source_target_pairs={{0,8},{8,16},{16,24},{1,9},{9,17},{17,25},{2,10},{10,18},{18,26},{... | collective-permute-start | bytes 294920 | tf_op jit(solution)/shard_map/ppermute | solution.py:306
  4.0 2.8 %fusion.1 = (f32[3,96,1,256]{3,2,1,0:T(1,128)S(1)}, f32[3,96,1,256]{3,2,1,0:T(1,128)S(1)}) fusion(f32[3,96,32,256]{3,2,1,0:T(8,128)} %velocity.1), kind=kLoop, calls=%fused_computation.16 | loop fusion | bytes 1179648 | tf_op jit(solution)/shard_map/slice | solution.py:325
  6.8 2.4 %collective-permute-start.2 = (f32[3,96,1,256]{3,2,1,0:T(1,128)S(1)}, f32[3,96,1,256]{3,2,1,0:T(1,128)S(1)}, u32[]{:S(2)}, u32[]{:S(2)}) collective-permute-start(f32[3,96,1,256]{3,2,1,0:T(1,128)S(1)} %get-tuple-element.17), channel_id=1, source_target_pairs={{0,1},{1,2},{2,3},{3,4},{4,5},{5,6},{6,7},{7,0},{8,9},{9,10},{10,1... | collective-permute-start | bytes 884744 | tf_op jit(solution)/shard_map/ppermute | solution.py:306
  9.2 3.1 %collective-permute-start.3 = (f32[3,96,1,256]{3,2,1,0:T(1,128)S(1)}, f32[3,96,1,256]{3,2,1,0:T(1,128)S(1)}, u32[]{:S(2)}, u32[]{:S(2)}) collective-permute-start(f32[3,96,1,256]{3,2,1,0:T(1,128)S(1)} %get-tuple-element.16), channel_id=1, source_target_pairs={{0,7},{1,0},{2,1},{3,2},{4,3},{5,4},{6,5},{7,6},{8,15},{9,8},{10,9... | collective-permute-start | bytes 884744 | tf_op jit(solution)/shard_map/ppermute | solution.py:306
  12.3 1.1 copy.33
  13.4 1.3 slice_reduce_fusion.hubs
  14.6 0.8 copy.25.tiles
  16.1 0.0 copy-start.5
  16.1 3.7 %copy-done.5 = f32[3,96,32,256]{3,2,1,0:T(8,128)S(1)} copy-done((f32[3,96,32,256]{3,2,1,0:T(8,128)S(1)}, f32[3,96,32,256]{3,2,1,0:T(8,128)}, u32[]{:S(2)}) %copy-start.5) | copy-done | bytes 9437208
  19.7 8.5 %load_sample.1 = (f32[3,96,32,256]{3,2,1,0:T(8,128)S(1)}, f32[64,3,256]{2,1,0:T(4,128)S(1)}, s32[65]{0:T(128)S(1)}) custom-call(f32[3,96,32,256]{3,2,1,0:T(8,128)S(1)} %copy-done.5, s32[64,3,256]{2,1,0:T(4,128)S(1)} %bitcast.30, s32[64]{0:T(128)S(1)} %slice_reduce_fusion.hubs, s32[64,2]{1,0:T(8,128)S(1)} %copy.25.tiles, s32[1]{0:T(128)} %copy.37.counts), custom_call_target="tpu_custom_call" | custom-call | flops 2000000000 | bytes 37748736 | tf_op jit(solution)/shard_map/load_sample/pallas_call | solution.py:327
  28.3 0.0 copy-start.2
  28.3 3.7 %copy-done.2 = f32[3,96,32,256]{3,2,1,0:T(8,128)} copy-done((f32[3,96,32,256]{3,2,1,0:T(8,128)}, f32[3,96,32,256]{3,2,1,0:T(8,128)S(1)}, u32[]{:S(2)}) %copy-start.2) | copy-done | bytes 9437208
  32.0 0.7 collective-permute-start.4
  32.7 4.0 %collective-permute-start.5 = (f32[64,3,256]{2,1,0:T(4,128)S(1)}, f32[64,3,256]{2,1,0:T(4,128)S(1)}, u32[]{:S(2)}, u32[]{:S(2)}) collective-permute-start(f32[64,3,256]{2,1,0:T(4,128)S(1)} %get-tuple-element.11.own), channel_id=1, source_target_pairs={{0,7},{1,0},{2,1},{3,2},{4,3},{5,4},{6,5},{7,6},{8,15},{9,8},{10,9... | collective-permute-start | bytes 589832 | tf_op jit(solution)/shard_map/ppermute | solution.py:306
  36.7 0.0 collective-permute-done.ghost_low
  36.7 1.3 collective-permute-start.1
  38.2 1.8 %collective-permute-done.1.ghost_high = f32[3,32,256]{2,1,0:T(8,128)S(1)} collective-permute-done((f32[3,32,256]{2,1,0:T(8,128)S(1)}, f32[3,32,256]{2,1,0:T(8,128)S(1)}, u32[]{:S(2)}, u32[]{:S(2)}) %collective-permute-start.1) | collective-permute-done | bytes 98336 | tf_op jit(solution)/shard_map/ppermute | solution.py:306
  39.9 0.0 collective-permute-done.2.south
  39.9 0.0 collective-permute-done.3.north
  39.9 0.0 copy-start.3
  40.0 3.7 %copy-done.3 = f32[3,96,32,256]{3,2,1,0:T(8,128)S(1)} copy-done((f32[3,96,32,256]{3,2,1,0:T(8,128)S(1)}, f32[3,96,32,256]{3,2,1,0:T(8,128)}, u32[]{:S(2)}) %copy-start.3) | copy-done | bytes 9437208
  43.6 11.6 %advance_first.1.field_in = f32[3,96,32,256]{3,2,1,0:T(8,128)S(1)} custom-call(f32[3,96,32,256]{3,2,1,0:T(8,128)S(1)} %copy-done.3, f32[3,32,256]{2,1,0:T(8,128)S(1)} %copy-done.6, f32[3,32,256]{2,1,0:T(8,128)S(1)} %collective-permute-done.ghost_low, f32[3,32,256]{2,1,0:T(8,128)S(1)} %collective-permute-done.1.ghost_high, ...), custom_call_target="tpu_custom_call" | custom-call | flops 1000000000 | bytes 37748736 | tf_op jit(solution)/shard_map/advance_first/pallas_call | solution.py:341
  55.2 0.0 collective-permute-done.4.low
  55.3 0.0 collective-permute-done.5.high
  55.3 7.5 %spread_section.1 = (f32[3,96,32,256]{3,2,1,0:T(8,128)S(1)}, f32[2,3,32,256]{3,2,1,0:T(8,128)S(1)}, f32[2,3,96,1,256]{4,3,2,1,0:T(1,128)S(1)}) custom-call(f32[3,96,32,256]{3,2,1,0:T(8,128)S(1)} %advance_first.1.field_in, s32[64,3,256]{2,1,0:T(4,128)S(1)} %bitcast.31, s32[64]{0:T(128)S(1)} %slice_reduce_fusion.hubs, ...), custom_call_target="tpu_custom_call", output_to_operand_aliasing={{0}: (0, {})} | custom-call | flops 2000000000 | bytes 37748736 | tf_op jit(solution)/shard_map/spread_section/pallas_call | solution.py:352
  62.8 1.3 collective-permute-start.6
  64.1 5.9 %sample.1.own = f32[64,3,256]{2,1,0:T(4,128)S(1)} custom-call(f32[3,96,32,256]{3,2,1,0:T(8,128)S(1)} %get-tuple-element.12.section.field, s32[64,3,256]{2,1,0:T(4,128)S(1)} %bitcast.32, s32[64]{0:T(128)S(1)} %slice_reduce_fusion.hubs, s32[65]{0:T(128)S(1)} %get-tuple-element.10.active), custom_call_target="tpu_custom_call" | custom-call | flops 2000000000 | bytes 37748736 | tf_op jit(solution)/shard_map/sample/pallas_call | solution.py:372
  70.1 3.6 %copy-done = f32[3,96,32,256]{3,2,1,0:T(8,128)} copy-done((f32[3,96,32,256]{3,2,1,0:T(8,128)}, f32[3,96,32,256]{3,2,1,0:T(8,128)S(1)}, u32[]{:S(2)}) %copy-start) | copy-done | bytes 9437208
  73.8 0.8 pad_maximum_fusion
  74.6 8.1 %all-to-all-start = ((f32[2,8,8,3,256]{4,2,3,0,1:T(8,128)}), f32[2,8,8,3,256]{4,2,3,0,1:T(8,128)S(1)}, u32[]{:S(2)}, u32[]{:S(2)}) async-start(f32[2,8,8,3,256]{4,2,3,0,1:T(8,128)} %pad_maximum_fusion), calls=%async_computation | async-start | bytes 786432 | tf_op jit(solution)/shard_map/all_to_all | solution.py:386
  82.6 0.4 slice_bitcast_fusion
  83.0 2.1 %collective-permute-start.8 = (f32[3,96,1,256]{3,2,1,0:T(1,128)S(1)}, f32[3,96,1,256]{3,2,1,0:T(1,128)S(1)}, u32[]{:S(2)}, u32[]{:S(2)}) collective-permute-start(f32[3,96,1,256]{3,2,1,0:T(1,128)S(1)} %get-tuple-element.21), channel_id=1, source_target_pairs={{0,1},{1,2},{2,3},{3,4},{4,5},{5,6},{6,7},{7,0},{8,9},{9,10},{10,1... | collective-permute-start | bytes 884744 | tf_op jit(solution)/shard_map/ppermute | solution.py:306
  85.1 2.8 %collective-permute-start.9 = (f32[3,96,1,256]{3,2,1,0:T(1,128)S(1)}, f32[3,96,1,256]{3,2,1,0:T(1,128)S(1)}, u32[]{:S(2)}, u32[]{:S(2)}) collective-permute-start(f32[3,96,1,256]{3,2,1,0:T(1,128)S(1)} %get-tuple-element.20), channel_id=1, source_target_pairs={{0,7},{1,0},{2,1},{3,2},{4,3},{5,4},{6,5},{7,6},{8,15},{9,8},{10,9... | collective-permute-start | bytes 884744 | tf_op jit(solution)/shard_map/ppermute | solution.py:306
  87.9 4.7 %collective-permute-start.11 = (f32[64,3,256]{2,1,0:T(4,128)S(1)}, f32[64,3,256]{2,1,0:T(4,128)S(1)}, u32[]{:S(2)}, u32[]{:S(2)}) collective-permute-start(f32[64,3,256]{2,1,0:T(4,128)S(1)} %sample.1.own), channel_id=1, source_target_pairs={{0,7},{1,0},{2,1},{3,2},{4,3},{5,4},{6,5},{7,6},{8,15},{9,8},{10,9... | collective-permute-start | bytes 589832 | tf_op jit(solution)/shard_map/ppermute | solution.py:306
  92.6 1.3 collective-permute-start.7
  93.9 0.1 fusion
  94.0 1.8 %collective-permute-done.7.ghost_high = f32[3,32,256]{2,1,0:T(8,128)S(1)} collective-permute-done((f32[3,32,256]{2,1,0:T(8,128)S(1)}, f32[3,32,256]{2,1,0:T(8,128)S(1)}, u32[]{:S(2)}, u32[]{:S(2)}) %collective-permute-start.7) | collective-permute-done | bytes 98336 | tf_op jit(solution)/shard_map/ppermute | solution.py:306
  95.8 0.6 collective-permute-done.8.south
  96.4 2.2 %collective-permute-done.9.north = f32[3,96,1,256]{3,2,1,0:T(1,128)S(1)} collective-permute-done((f32[3,96,1,256]{3,2,1,0:T(1,128)S(1)}, f32[3,96,1,256]{3,2,1,0:T(1,128)S(1)}, u32[]{:S(2)}, u32[]{:S(2)}) %collective-permute-start.9) | collective-permute-done | bytes 294944 | tf_op jit(solution)/shard_map/ppermute | solution.py:306
  98.5 3.7 %copy-done.1 = f32[3,96,32,256]{3,2,1,0:T(8,128)S(1)} copy-done((f32[3,96,32,256]{3,2,1,0:T(8,128)S(1)}, f32[3,96,32,256]{3,2,1,0:T(8,128)}, u32[]{:S(2)}) %copy-start.1) | copy-done | bytes 9437208
  102.2 3.7 %copy-done.4 = f32[3,96,32,256]{3,2,1,0:T(8,128)S(1)} copy-done((f32[3,96,32,256]{3,2,1,0:T(8,128)S(1)}, f32[3,96,32,256]{3,2,1,0:T(8,128)}, u32[]{:S(2)}) %copy-start.4) | copy-done | bytes 9437208
  105.9 11.8 %advance_second.1.field_in = f32[3,96,32,256]{3,2,1,0:T(8,128)S(1)} custom-call(f32[3,96,32,256]{3,2,1,0:T(8,128)S(1)} %copy-done.1, f32[3,96,32,256]{3,2,1,0:T(8,128)S(1)} %copy-done.4, f32[3,32,256]{2,1,0:T(8,128)S(1)} %copy-done.6, f32[3,32,256]{2,1,0:T(8,128)S(1)} %collective-permute-done.6.ghost_low, ...), custom_call_target="tpu_custom_call" | custom-call | flops 1000000000 | bytes 37748736 | tf_op jit(solution)/shard_map/advance_second/pallas_call | solution.py:394
  117.6 0.0 collective-permute-done.10.low
  117.7 0.0 collective-permute-done.11.high
  117.7 11.0 %spread_next.1 = (f32[3,96,32,256]{3,2,1,0:T(8,128)S(1)}, f32[3,96,32,256]{3,2,1,0:T(8,128)}) custom-call(f32[3,96,32,256]{3,2,1,0:T(8,128)S(1)} %advance_second.1.field_in, s32[64,3,256]{2,1,0:T(4,128)S(1)} %bitcast.33, s32[64]{0:T(128)S(1)} %slice_reduce_fusion.hubs, s32[65]{0:T(128)S(1)} %get-tuple-element.10.active, ...), custom_call_target="tpu_custom_call", output_to_operand_aliasing={{0}: (0, {})} | custom-call | flops 2000000000 | bytes 37748736 | tf_op jit(solution)/shard_map/spread_next/pallas_call | solution.py:405
  128.7 32.6 %all_gather.3 = f32[64,3,256]{2,0,1:T(8,128)S(1)} all-gather(f32[8,3,256]{2,0,1:T(8,128)S(1)} %broadcast_multiply_fusion), channel_id=1, replica_groups=mesh['gx'=4,'gy'=8] {'gy'}, dimensions={0}, use_global_device_ids=true | all-gather | bytes 221184 | tf_op jit(solution)/shard_map/all_gather | solution.py:392
  161.4 0.7 copy.38
  (20 shorter events, 0.2 us)
Async XLA Ops:
  0.6 37.4 %copy-start.7 = (f32[1,64,256]{2,1,0:T(8,128)S(1)}, f32[1,64,256]{2,1,0:T(8,128)}, u32[]{:S(2)}) copy-start(f32[1,64,256]{2,1,0:T(8,128)} %param.10) | copy-start | bytes 196612
  0.6 39.3 %copy-start.6 = (f32[3,32,256]{2,1,0:T(8,128)S(1)}, f32[3,32,256]{2,1,0:T(8,128)}, u32[]{:S(2)}) copy-start(f32[3,32,256]{2,1,0:T(8,128)} %inflow.3) | copy-start | bytes 294916
  1.6 35.1 %collective-permute-start = (f32[3,32,256]{2,1,0:T(8,128)S(1)}, f32[3,32,256]{2,1,0:T(8,128)S(1)}, u32[]{:S(2)}, u32[]{:S(2)}) collective-permute-start(f32[3,32,256]{2,1,0:T(8,128)S(1)} %get-tuple-element.19), channel_id=1, source_target_pairs={{0,8},{8,16},{16,24},{1,9},{9,17},{17,25},{2,10},{10,18},{18,26},{... | collective-permute-start | bytes 294920 | tf_op jit(solution)/shard_map/ppermute | solution.py:306
  6.8 33.1 %collective-permute-start.2 = (f32[3,96,1,256]{3,2,1,0:T(1,128)S(1)}, f32[3,96,1,256]{3,2,1,0:T(1,128)S(1)}, u32[]{:S(2)}, u32[]{:S(2)}) collective-permute-start(f32[3,96,1,256]{3,2,1,0:T(1,128)S(1)} %get-tuple-element.17), channel_id=1, source_target_pairs={{0,1},{1,2},{2,3},{3,4},{4,5},{5,6},{6,7},{7,0},{8,9},{9,10},{10,1... | collective-permute-start | bytes 884744 | tf_op jit(solution)/shard_map/ppermute | solution.py:306
  9.2 30.7 %collective-permute-start.3 = (f32[3,96,1,256]{3,2,1,0:T(1,128)S(1)}, f32[3,96,1,256]{3,2,1,0:T(1,128)S(1)}, u32[]{:S(2)}, u32[]{:S(2)}) collective-permute-start(f32[3,96,1,256]{3,2,1,0:T(1,128)S(1)} %get-tuple-element.16), channel_id=1, source_target_pairs={{0,7},{1,0},{2,1},{3,2},{4,3},{5,4},{6,5},{7,6},{8,15},{9,8},{10,9... | collective-permute-start | bytes 884744 | tf_op jit(solution)/shard_map/ppermute | solution.py:306
  16.1 3.7 %copy-start.5 = (f32[3,96,32,256]{3,2,1,0:T(8,128)S(1)}, f32[3,96,32,256]{3,2,1,0:T(8,128)}, u32[]{:S(2)}) copy-start(f32[3,96,32,256]{3,2,1,0:T(8,128)} %velocity.1) | copy-start | bytes 28311556
  28.3 3.7 %copy-start.2 = (f32[3,96,32,256]{3,2,1,0:T(8,128)}, f32[3,96,32,256]{3,2,1,0:T(8,128)S(1)}, u32[]{:S(2)}) copy-start(f32[3,96,32,256]{3,2,1,0:T(8,128)S(1)} %get-tuple-element.9.field) | copy-start | bytes 28311556
  32.0 23.2 %collective-permute-start.4 = (f32[64,3,256]{2,1,0:T(4,128)S(1)}, f32[64,3,256]{2,1,0:T(4,128)S(1)}, u32[]{:S(2)}, u32[]{:S(2)}) collective-permute-start(f32[64,3,256]{2,1,0:T(4,128)S(1)} %get-tuple-element.11.own), channel_id=1, source_target_pairs={{0,1},{1,2},{2,3},{3,4},{4,5},{5,6},{6,7},{7,0},{8,9},{9,10},{10,1... | collective-permute-start | bytes 589832 | tf_op jit(solution)/shard_map/ppermute | solution.py:306
  32.7 22.5 %collective-permute-start.5 = (f32[64,3,256]{2,1,0:T(4,128)S(1)}, f32[64,3,256]{2,1,0:T(4,128)S(1)}, u32[]{:S(2)}, u32[]{:S(2)}) collective-permute-start(f32[64,3,256]{2,1,0:T(4,128)S(1)} %get-tuple-element.11.own), channel_id=1, source_target_pairs={{0,7},{1,0},{2,1},{3,2},{4,3},{5,4},{6,5},{7,6},{8,15},{9,8},{10,9... | collective-permute-start | bytes 589832 | tf_op jit(solution)/shard_map/ppermute | solution.py:306
  36.7 3.2 %collective-permute-start.1 = (f32[3,32,256]{2,1,0:T(8,128)S(1)}, f32[3,32,256]{2,1,0:T(8,128)S(1)}, u32[]{:S(2)}, u32[]{:S(2)}) collective-permute-start(f32[3,32,256]{2,1,0:T(8,128)S(1)} %get-tuple-element.18), channel_id=1, source_target_pairs={{8,0},{16,8},{24,16},{9,1},{17,9},{25,17},{10,2},{18,10},{26,18},{... | collective-permute-start | bytes 294920 | tf_op jit(solution)/shard_map/ppermute | solution.py:306
  39.9 3.7 %copy-start.3 = (f32[3,96,32,256]{3,2,1,0:T(8,128)S(1)}, f32[3,96,32,256]{3,2,1,0:T(8,128)}, u32[]{:S(2)}) copy-start(f32[3,96,32,256]{3,2,1,0:T(8,128)} %copy-done.2) | copy-start | bytes 28311556
  62.8 29.8 %collective-permute-start.6 = (f32[3,32,256]{2,1,0:T(8,128)S(1)}, f32[3,32,256]{2,1,0:T(8,128)S(1)}, u32[]{:S(2)}, u32[]{:S(2)}) collective-permute-start(f32[3,32,256]{2,1,0:T(8,128)S(1)} %get-tuple-element.23), channel_id=1, source_target_pairs={{0,8},{8,16},{16,24},{1,9},{9,17},{17,25},{2,10},{10,18},{18,26},{... | collective-permute-start | bytes 294920 | tf_op jit(solution)/shard_map/ppermute | solution.py:306
  70.1 3.6 %copy-start = (f32[3,96,32,256]{3,2,1,0:T(8,128)}, f32[3,96,32,256]{3,2,1,0:T(8,128)S(1)}, u32[]{:S(2)}) copy-start(f32[3,96,32,256]{3,2,1,0:T(8,128)S(1)} %get-tuple-element.12.section.field) | copy-start | bytes 28311556
  74.6 54.1 %all-to-all-start = ((f32[2,8,8,3,256]{4,2,3,0,1:T(8,128)}), f32[2,8,8,3,256]{4,2,3,0,1:T(8,128)S(1)}, u32[]{:S(2)}, u32[]{:S(2)}) async-start(f32[2,8,8,3,256]{4,2,3,0,1:T(8,128)} %pad_maximum_fusion), calls=%async_computation | async-start | bytes 786432 | tf_op jit(solution)/shard_map/all_to_all | solution.py:386
  83.0 13.3 %collective-permute-start.8 = (f32[3,96,1,256]{3,2,1,0:T(1,128)S(1)}, f32[3,96,1,256]{3,2,1,0:T(1,128)S(1)}, u32[]{:S(2)}, u32[]{:S(2)}) collective-permute-start(f32[3,96,1,256]{3,2,1,0:T(1,128)S(1)} %get-tuple-element.21), channel_id=1, source_target_pairs={{0,1},{1,2},{2,3},{3,4},{4,5},{5,6},{6,7},{7,0},{8,9},{9,10},{10,1... | collective-permute-start | bytes 884744 | tf_op jit(solution)/shard_map/ppermute | solution.py:306
  85.1 13.4 %collective-permute-start.9 = (f32[3,96,1,256]{3,2,1,0:T(1,128)S(1)}, f32[3,96,1,256]{3,2,1,0:T(1,128)S(1)}, u32[]{:S(2)}, u32[]{:S(2)}) collective-permute-start(f32[3,96,1,256]{3,2,1,0:T(1,128)S(1)} %get-tuple-element.20), channel_id=1, source_target_pairs={{0,7},{1,0},{2,1},{3,2},{4,3},{5,4},{6,5},{7,6},{8,15},{9,8},{10,9... | collective-permute-start | bytes 884744 | tf_op jit(solution)/shard_map/ppermute | solution.py:306
  87.9 29.8 %collective-permute-start.10 = (f32[64,3,256]{2,1,0:T(4,128)S(1)}, f32[64,3,256]{2,1,0:T(4,128)S(1)}, u32[]{:S(2)}, u32[]{:S(2)}) collective-permute-start(f32[64,3,256]{2,1,0:T(4,128)S(1)} %sample.1.own), channel_id=1, source_target_pairs={{0,1},{1,2},{2,3},{3,4},{4,5},{5,6},{6,7},{7,0},{8,9},{9,10},{10,1... | collective-permute-start | bytes 589832 | tf_op jit(solution)/shard_map/ppermute | solution.py:306
  87.9 29.8 %collective-permute-start.11 = (f32[64,3,256]{2,1,0:T(4,128)S(1)}, f32[64,3,256]{2,1,0:T(4,128)S(1)}, u32[]{:S(2)}, u32[]{:S(2)}) collective-permute-start(f32[64,3,256]{2,1,0:T(4,128)S(1)} %sample.1.own), channel_id=1, source_target_pairs={{0,7},{1,0},{2,1},{3,2},{4,3},{5,4},{6,5},{7,6},{8,15},{9,8},{10,9... | collective-permute-start | bytes 589832 | tf_op jit(solution)/shard_map/ppermute | solution.py:306
  92.6 3.2 %collective-permute-start.7 = (f32[3,32,256]{2,1,0:T(8,128)S(1)}, f32[3,32,256]{2,1,0:T(8,128)S(1)}, u32[]{:S(2)}, u32[]{:S(2)}) collective-permute-start(f32[3,32,256]{2,1,0:T(8,128)S(1)} %get-tuple-element.22), channel_id=1, source_target_pairs={{8,0},{16,8},{24,16},{9,1},{17,9},{25,17},{10,2},{18,10},{26,18},{... | collective-permute-start | bytes 294920 | tf_op jit(solution)/shard_map/ppermute | solution.py:306
  98.5 3.7 %copy-start.1 = (f32[3,96,32,256]{3,2,1,0:T(8,128)S(1)}, f32[3,96,32,256]{3,2,1,0:T(8,128)}, u32[]{:S(2)}) copy-start(f32[3,96,32,256]{3,2,1,0:T(8,128)} %copy-done) | copy-start | bytes 28311556
  102.2 3.7 %copy-start.4 = (f32[3,96,32,256]{3,2,1,0:T(8,128)S(1)}, f32[3,96,32,256]{3,2,1,0:T(8,128)}, u32[]{:S(2)}) copy-start(f32[3,96,32,256]{3,2,1,0:T(8,128)} %copy-done.2) | copy-start | bytes 28311556
